TPU v7x, 32 devices: a whole 2x2x4 slice. The times are simulated.
32 devices in a mesh: energy: 8 (over y, x, core), mom: 4 (over z).
Axes of the slice: x: 2, y: 2, z: 4, core: 2. Of those that a mesh axis runs over, the one named last changes fastest.
Arguments:
- green_ret: bfloat16 [8, 4, 12, 3, 2, 128, 128], P('energy', 'mom'), may hold values from -0.5 to 0.5
- sigma_in: bfloat16 [8, 4, 12, 2, 128, 128], P('energy', 'mom'), may hold values from -6 to 6
- coupling: bfloat16 [4, 128, 128], replicated, may hold values from -0.5 to 0.5
- pattern: int32 [12], replicated, may hold values from 0 to 3
- neighbours: int32 [4, 3], P('mom'), may hold values from -1 to 1
- offsets: int32 [32], replicated, may hold values from -8 to 8, as said below
- tap_weight: float32 [32], replicated, may hold values from 0.005 to 0.04
Outputs:
- self_energy: bfloat16 [8, 4, 2, 1536, 128], P(None, 'mom', None, 'energy')
Inputs may be any that keep to these rules, and one draw needn't show every extreme that they name: `offsets`: both ends of the range are taken by some tap.
All inputs are finite; a program needn't handle non-finite values.
Results may differ from a plain program's by a relative error of at most 0.0081.
Values may be sent and summed in bfloat16 or wider, within the bound.
A program may use at most 64 MiB of HBM per device.

v0:
```python
import jax
import jax.numpy as jnp
from jax import lax
from jax.sharding import PartitionSpec as P


def shifted(value, axis, steps):
    count = lax.axis_size(axis)
    pairs = [(source, (source + steps) % count) for source in range(count)]
    return lax.ppermute(value, axis, pairs)


def batched(left, right):
    return jnp.einsum("sab,sbc->sac", left, right, preferred_element_type=jnp.float32)


def batched_adjoint(left, right):
    return jnp.einsum("sab,scb->sac", left, right, preferred_element_type=jnp.float32)


def slab_lesser(green, padded, slab_coupling, first, last):
    orbitals = green.shape[-1]
    count = last - first
    couple = slab_coupling[first:last]
    total_real = jnp.zeros((count, orbitals, orbitals), jnp.float32)
    total_imag = jnp.zeros((count, orbitals, orbitals), jnp.float32)
    for term in range(3):
        near = padded[first + term : last + term]
        block = green[first:last, term]
        coupled_real = batched(couple, block[:, 0]).astype(jnp.bfloat16)
        coupled_imag = batched(couple, block[:, 1]).astype(jnp.bfloat16)
        left_real = (batched(coupled_real, near[:, 0]) - batched(coupled_imag, near[:, 1])).astype(
            jnp.bfloat16
        )
        left_imag = (batched(coupled_real, near[:, 1]) + batched(coupled_imag, near[:, 0])).astype(
            jnp.bfloat16
        )
        total_real = (
            total_real
            + batched_adjoint(left_real, coupled_real)
            + batched_adjoint(left_imag, coupled_imag)
        )
        total_imag = (
            total_imag
            + batched_adjoint(left_imag, coupled_real)
            - batched_adjoint(left_real, coupled_imag)
        )
    rows = count * orbitals
    return jnp.stack(
        [total_real.reshape(rows, orbitals), total_imag.reshape(rows, orbitals)]
    ).astype(jnp.bfloat16)


def shards(green_ret, sigma_in, coupling, pattern, neighbours, offsets, tap_weight):
    e_local = green_ret.shape[0]
    energies = e_local * lax.axis_size("energy")
    slabs = green_ret.shape[2]
    half = slabs // 2
    kinds = coupling.shape[0]
    onehot = (pattern[:, None] == jnp.arange(kinds, dtype=jnp.int32)[None, :]).astype(jnp.bfloat16)
    slab_coupling = jnp.dot(onehot, coupling.reshape(kinds, -1), preferred_element_type=jnp.float32)
    slab_coupling = slab_coupling.astype(jnp.bfloat16).reshape(
        slabs, coupling.shape[1], coupling.shape[2]
    )
    weights = [jnp.sum((neighbours[0] == side).astype(jnp.float32)) for side in (-1, 0, 1)]
    index = jnp.arange(energies, dtype=jnp.int32)
    hit = index[None, :, None] == index[:, None, None] - offsets[None, None, :]
    banded = jnp.sum(
        jnp.where(hit, tap_weight[None, None, :], jnp.zeros((), jnp.float32)), axis=2
    ).astype(jnp.bfloat16)
    green = green_ret[0, 0]
    padded = jnp.pad(sigma_in[0, 0], ((1, 1), (0, 0), (0, 0), (0, 0)))
    pieces = []
    for first in (0, half):
        piece = slab_lesser(green, padded, slab_coupling, first, first + half)
        below = shifted(piece, "mom", 1)
        above = shifted(piece, "mom", -1)
        total = weights[0] * below.astype(jnp.float32) + weights[1] * piece.astype(jnp.float32)
        pieces.append((total + weights[2] * above.astype(jnp.float32)).astype(jnp.bfloat16))
    mixed_parts = [jnp.concatenate(pieces, axis=1)]
    mixed = jnp.stack(mixed_parts)
    result = jnp.einsum(
        "ef,fcrk->ecrk",
        banded,
        lax.all_to_all(mixed, "energy", split_axis=2, concat_axis=0, tiled=True),
        preferred_element_type=jnp.float32,
    ).astype(jnp.bfloat16)
    return result[:, None]


def solution(mesh):
    return jax.shard_map(
        shards,
        mesh=mesh,
        in_specs=(
            P("energy", "mom", None, None, None, None, None),
            P("energy", "mom", None, None, None, None),
            P(),
            P(),
            P("mom", None),
            P(),
            P(),
        ),
        out_specs=P(None, "mom", None, "energy", None),
        check_vma=False,
    )
```

profile of v0, /device:TPU:0, one launch (start us, length us, event | category | flops | bytes accessed | tf_op | source)
XLA Modules:
  0.0 78.1 jit_solution(17315510375331789014)
XLA Ops:
  0.0 1.8 %copy.124 = bf16[1,1,12,3,2,128,128]{6,5,2,4,3,1,0:T(8,128)(2,1)S(1)} copy(bf16[1,1,12,3,2,128,128]{6,5,4,3,2,1,0:T(8,128)(2,1)} %param.7) | data formatting | bytes 4718592 | tf_op args[0]
  1.8 0.3 slice_bitcast_fusion.6
  2.1 0.6 copy-done.1
  2.7 0.3 convolution_convert_fusion
  4.6 0.3 slice_bitcast_fusion.5
  5.9 0.3 fusion.86
  6.4 0.3 fusion.85
  6.7 0.3 convolution_subtract_fusion.2
  8.2 0.3 convolution_add_fusion.8
  8.4 0.3 convolution_add_fusion.1
  8.7 0.3 convolution_subtract_fusion.1
  9.0 0.3 convolution_add_fusion.7
  9.2 0.3 convolution_add_fusion.5
  9.5 0.3 convolution_add_fusion
  9.8 0.3 fusion.16
  10.0 0.3 convolution_add_fusion.4
  10.3 0.3 fusion.15
  10.6 5.1 %collective-permute-start.3 = (bf16[2,768,128]{2,1,0:T(8,128)(2,1)S(1)}, bf16[2,768,128]{2,1,0:T(8,128)(2,1)S(1)}, u32[]{:S(2)}, u32[]{:S(2)}) collective-permute-start(bf16[2,768,128]{2,1,0:T(8,128)(2,1)S(1)} %pad_maximum_fusion.1), channel_id=1, source_target_pairs={{0,3},{1,0},{2,1},{3,2},{4,7},{5,4},{6,5},{7,6},{8,11},{9,8},{10,9... | collective-permute-start | bytes 1179656 | tf_op jit(solution)/shard_map/ppermute | solution.py:10
  17.5 0.3 fusion.84
  18.0 0.3 fusion.83
  18.2 0.3 convolution_subtract_fusion.8
  18.5 0.2 fusion.35
  18.7 0.2 fusion.36
  18.9 0.2 fusion.4
  19.2 0.2 fusion.3
  19.8 0.2 fusion.6
  20.0 0.2 fusion.5
  20.2 0.3 convolution_add_fusion.18
  20.5 0.3 convolution_add_fusion.11
  20.8 0.3 convolution_subtract_fusion.7
  21.0 0.3 convolution_add_fusion.17
  21.3 0.3 convolution_add_fusion.15
  21.5 0.3 convolution_add_fusion.10
  21.8 0.3 fusion.8
  22.1 0.3 convolution_add_fusion.14
  22.4 0.3 fusion.7
  22.7 3.9 %collective-permute-start.1 = (bf16[2,768,128]{2,1,0:T(8,128)(2,1)S(1)}, bf16[2,768,128]{2,1,0:T(8,128)(2,1)S(1)}, u32[]{:S(2)}, u32[]{:S(2)}) collective-permute-start(bf16[2,768,128]{2,1,0:T(8,128)(2,1)S(1)} %pad_maximum_fusion), channel_id=1, source_target_pairs={{0,3},{1,0},{2,1},{3,2},{4,7},{5,4},{6,5},{7,6},{8,11},{9,8},{10,9... | collective-permute-start | bytes 1179656 | tf_op jit(solution)/shard_map/ppermute | solution.py:10
  26.6 0.6 fusion.60
  27.2 7.4 %collective-permute-done.2 = bf16[2,768,128]{2,1,0:T(8,128)(2,1)S(1)} collective-permute-done((bf16[2,768,128]{2,1,0:T(8,128)(2,1)S(1)}, bf16[2,768,128]{2,1,0:T(8,128)(2,1)S(1)}, u32[]{:S(2)}, u32[]{:S(2)}) %collective-permute-start.2) | collective-permute-done | bytes 393248 | tf_op jit(solution)/shard_map/ppermute | solution.py:10
  34.6 2.1 %add_convert_fusion = bf16[2,768,128]{2,1,0:T(8,128)(2,1)S(1)} fusion(bf16[2,768,128]{2,1,0:T(8,128)(2,1)S(1)} %collective-permute-done.3, bf16[2,768,128]{2,1,0:T(8,128)(2,1)S(1)} %collective-permute-done.2, f32[]{:T(128)} %get-tuple-element.6, f32[]{:T(128)} %get-tuple-element.7, f32[]{:T(128)} %get-tuple-element.5, bf16[1,768,128]{2,1,0:T(8,128)(2,1)S(1)} %bitcast.254, ...), kind=kLoop, calls=%fused_computation.71 | loop fusion | flops 1966080 | bytes 1572876 | tf_op jit(solution)/shard_map/convert_element_type | solution.py:79
  36.7 5.5 %collective-permute-done.1 = bf16[2,768,128]{2,1,0:T(8,128)(2,1)S(1)} collective-permute-done((bf16[2,768,128]{2,1,0:T(8,128)(2,1)S(1)}, bf16[2,768,128]{2,1,0:T(8,128)(2,1)S(1)}, u32[]{:S(2)}, u32[]{:S(2)}) %collective-permute-start.1) | collective-permute-done | bytes 393248 | tf_op jit(solution)/shard_map/ppermute | solution.py:10
  42.1 8.2 %collective-permute-done = bf16[2,768,128]{2,1,0:T(8,128)(2,1)S(1)} collective-permute-done((bf16[2,768,128]{2,1,0:T(8,128)(2,1)S(1)}, bf16[2,768,128]{2,1,0:T(8,128)(2,1)S(1)}, u32[]{:S(2)}, u32[]{:S(2)}) %collective-permute-start) | collective-permute-done | bytes 393248 | tf_op jit(solution)/shard_map/ppermute | solution.py:10
  50.3 2.1 %add_convert_fusion.1 = bf16[2,768,128]{2,1,0:T(8,128)(2,1)S(1)} fusion(bf16[2,768,128]{2,1,0:T(8,128)(2,1)S(1)} %collective-permute-done.1, bf16[2,768,128]{2,1,0:T(8,128)(2,1)S(1)} %collective-permute-done, f32[]{:T(128)} %get-tuple-element.6, f32[]{:T(128)} %get-tuple-element.7, f32[]{:T(128)} %get-tuple-element.5, bf16[1,768,128]{2,1,0:T(8,128)(2,1)S(1)} %bitcast.258, ...), kind=kLoop, calls=%fused_computation.72 | loop fusion | flops 1966080 | bytes 1572876 | tf_op jit(solution)/shard_map/convert_element_type | solution.py:79
  52.5 7.3 %copy.55 = bf16[1,2,1536,128]{3,1,0,2:T(2,128)(2,1)} copy(bf16[1,2,1536,128]{3,2,1,0:T(8,128)(2,1)S(1)} %maximum_bitcast_fusion) | data formatting | bytes 1572864 | tf_op jit(solution)/shard_map/stack | solution.py:81
  59.7 3.7 %all-to-all-start = ((bf16[1,2,1536,128]{3,1,0,2:T(2,128)(2,1)}), bf16[1,2,1536,128]{3,1,0,2:T(2,128)(2,1)S(1)}, u32[]{:S(2)}, u32[]{:S(2)}) async-start(bf16[1,2,1536,128]{3,1,0,2:T(2,128)(2,1)} %copy.55), calls=%async_computation | async-start | bytes 1572864 | tf_op jit(solution)/shard_map/all_to_all | solution.py:85
  63.6 12.5 %all-to-all-done = bf16[1,2,1536,128]{3,1,0,2:T(2,128)(2,1)S(1)} async-done(((bf16[1,2,1536,128]{3,1,0,2:T(2,128)(2,1)}), bf16[1,2,1536,128]{3,1,0,2:T(2,128)(2,1)S(1)}, u32[]{:S(2)}, u32[]{:S(2)}) %all-to-all-start) | async-done | bytes 786464 | tf_op jit(solution)/shard_map/all_to_all | solution.py:85
  76.0 1.0 %fusion = bf16[8,1,2,192,128]{4,0,3,2,1:T(8,128)(2,1)S(1)} fusion(bf16[1,2,8,192,128]{4,1,3,2,0:T(2,128)(2,1)S(1)} %bitcast.252, bf16[8,8]{1,0:T(8,128)(2,1)S(1)} %select_reduce_fusion), kind=kOutput, calls=%fused_computation.3 | convolution fusion | flops 6684672 | bytes 1572992 | tf_op jit(solution)/shard_map/ef,fcrk->ecrk/dot_general | solution.py:82
  77.0 1.1 %copy.58 = bf16[8,1,2,192,128]{4,3,2,1,0:T(8,128)(2,1)} copy(bf16[8,1,2,192,128]{4,0,3,2,1:T(8,128)(2,1)S(1)} %fusion) | data formatting | bytes 1572864 | tf_op jit(solution)/shard_map/broadcast_in_dim | solution.py:88
  (51 shorter events, 6.4 us)
Async XLA Ops:
  1.8 0.9 %copy-start.1 = (bf16[4,128,128]{2,1,0:T(8,128)(2,1)S(1)}, bf16[4,128,128]{2,1,0:T(8,128)(2,1)}, u32[]{:S(2)}) copy-start(bf16[4,128,128]{2,1,0:T(8,128)(2,1)} %param.9) | copy-start | bytes 393220
  1.8 0.9 %copy-start.5 = (s32[12]{0:T(128)S(1)}, s32[12]{0:T(128)}, u32[]{:S(2)}) copy-start(s32[12]{0:T(128)} %param.10) | copy-start | bytes 148
  3.4 1.1 %copy-start = (bf16[1,1,12,2,128,128]{5,4,3,2,1,0:T(8,128)(2,1)S(1)}, bf16[1,1,12,2,128,128]{5,4,3,2,1,0:T(8,128)(2,1)}, u32[]{:S(2)}) copy-start(bf16[1,1,12,2,128,128]{5,4,3,2,1,0:T(8,128)(2,1)} %param.8) | copy-start | bytes 2359300
  10.6 16.5 %collective-permute-start.3 = (bf16[2,768,128]{2,1,0:T(8,128)(2,1)S(1)}, bf16[2,768,128]{2,1,0:T(8,128)(2,1)S(1)}, u32[]{:S(2)}, u32[]{:S(2)}) collective-permute-start(bf16[2,768,128]{2,1,0:T(8,128)(2,1)S(1)} %pad_maximum_fusion.1), channel_id=1, source_target_pairs={{0,3},{1,0},{2,1},{3,2},{4,7},{5,4},{6,5},{7,6},{8,11},{9,8},{10,9... | collective-permute-start | bytes 1179656 | tf_op jit(solution)/shard_map/ppermute | solution.py:10
  15.7 18.9 %collective-permute-start.2 = (bf16[2,768,128]{2,1,0:T(8,128)(2,1)S(1)}, bf16[2,768,128]{2,1,0:T(8,128)(2,1)S(1)}, u32[]{:S(2)}, u32[]{:S(2)}) collective-permute-start(bf16[2,768,128]{2,1,0:T(8,128)(2,1)S(1)} %pad_maximum_fusion.1), channel_id=1, source_target_pairs={{0,1},{1,2},{2,3},{3,0},{4,5},{5,6},{6,7},{7,4},{8,9},{9,10},{10,1... | collective-permute-start | bytes 1179656 | tf_op jit(solution)/shard_map/ppermute | solution.py:10
  22.1 4.5 %copy-start.3 = (s32[1,3]{1,0:T(1,128)S(1)}, s32[1,3]{1,0:T(1,128)}, u32[]{:S(2)}) copy-start(s32[1,3]{1,0:T(1,128)} %param.11) | copy-start | bytes 40
  22.7 19.5 %collective-permute-start.1 = (bf16[2,768,128]{2,1,0:T(8,128)(2,1)S(1)}, bf16[2,768,128]{2,1,0:T(8,128)(2,1)S(1)}, u32[]{:S(2)}, u32[]{:S(2)}) collective-permute-start(bf16[2,768,128]{2,1,0:T(8,128)(2,1)S(1)} %pad_maximum_fusion), channel_id=1, source_target_pairs={{0,3},{1,0},{2,1},{3,2},{4,7},{5,4},{6,5},{7,6},{8,11},{9,8},{10,9... | collective-permute-start | bytes 1179656 | tf_op jit(solution)/shard_map/ppermute | solution.py:10
  26.5 23.8 %collective-permute-start = (bf16[2,768,128]{2,1,0:T(8,128)(2,1)S(1)}, bf16[2,768,128]{2,1,0:T(8,128)(2,1)S(1)}, u32[]{:S(2)}, u32[]{:S(2)}) collective-permute-start(bf16[2,768,128]{2,1,0:T(8,128)(2,1)S(1)} %pad_maximum_fusion), channel_id=1, source_target_pairs={{0,1},{1,2},{2,3},{3,0},{4,5},{5,6},{6,7},{7,4},{8,9},{9,10},{10,1... | collective-permute-start | bytes 1179656 | tf_op jit(solution)/shard_map/ppermute | solution.py:10
  52.4 11.0 %copy-start.2 = (s32[32]{0:T(128)S(1)}, s32[32]{0:T(128)}, u32[]{:S(2)}) copy-start(s32[32]{0:T(128)} %param.12) | copy-start | bytes 388
  52.5 11.0 %copy-start.4 = (f32[32]{0:T(128)S(1)}, f32[32]{0:T(128)}, u32[]{:S(2)}) copy-start(f32[32]{0:T(128)} %param.13) | copy-start | bytes 388
  59.7 16.3 %all-to-all-start = ((bf16[1,2,1536,128]{3,1,0,2:T(2,128)(2,1)}), bf16[1,2,1536,128]{3,1,0,2:T(2,128)(2,1)S(1)}, u32[]{:S(2)}, u32[]{:S(2)}) async-start(bf16[1,2,1536,128]{3,1,0,2:T(2,128)(2,1)} %copy.55), calls=%async_computation | async-start | bytes 1572864 | tf_op jit(solution)/shard_map/all_to_all | solution.py:85
where the time goes:
time: 78.4 us; the launch traced here: 78.1 us
  waiting for transfers between devices  33.6 us (43%)
  matrix products  14.8 us (19%)
  starting transfers between devices  12.7 us (16%)
  local copies, waits for them, and re-layouts  11.6 us (15%)
  other arithmetic  4.95 us (6%)
    ppermute x4, waiting for transfers between devices, shifted(): return lax.ppermute(value, axis, pairs)  21.1 us
    all_to_all x1, waiting for transfers between devices, shards(): lax.all_to_all(mixed, 'energy', split_axis=2, concat_axis=0, tiled=True)  12.5 us
    ppermute x4, starting transfers between devices, shifted(): return lax.ppermute(value, axis, pairs)  8.98 us
    another operation x1, local copies, waits for them, and re-layouts, shards(): mixed = jnp.stack(mixed_parts)  7.26 us
    dot_general x36, matrix products, batched(): jnp.einsum('sab,sbc->sac', left, right, preferred_element_type=jnp.float32)  7.14 us
    dot_general x24, matrix products, batched_adjoint(): jnp.einsum('sab,scb->sac', left, right, preferred_element_type=jnp.float32)  6.33 us
    convert_element_type x2, other arithmetic, shards(): (total + weights[2] * above.astype(jnp.float32)).astype(jnp.bfloat16)  4.11 us
    all_to_all x1, starting transfers between devices, shards(): lax.all_to_all(mixed, 'energy', split_axis=2, concat_axis=0, tiled=True)  3.71 us
  transfers between devices with their start and end apart: 5, of which 4 were waited for; matrix products, arithmetic and copies ran while one was open for 12% of the time, Pallas kernels for 0%

commit v1 on v0

--- a/solution.py
+++ b/solution.py
@@ -82,7 +82,12 @@
     result = jnp.einsum(
         "ef,fcrk->ecrk",
         banded,
-        lax.all_to_all(mixed, "energy", split_axis=2, concat_axis=0, tiled=True),
+        jnp.concatenate(
+            lax.all_to_all(
+                jnp.stack(jnp.split(mixed, lax.axis_size("energy"), axis=2)), "energy", 0, 0
+            ),
+            axis=0,
+        ),
         preferred_element_type=jnp.float32,
     ).astype(jnp.bfloat16)
     return result[:, None]

time: 78.4 us -> 75.9 us (0.968)
  local copies, waits for them, and re-layouts: 11.6 us -> 9.49 us
    another operation x1, local copies, waits for them, and re-layouts: 7.26 us -> 0.65 us  [shards(): jnp.stack(jnp.split(mixed, lax.axis_size('energy'), axis=2))]
    unnamed x15 -> x22, local copies, waits for them, and re-layouts: 2.72 us -> 7.25 us
  transfers between devices with their start and end apart: 5 -> 5, of which waited for: 4 -> 4; matrix products, arithmetic and copies ran while one was open for 12% -> 13% of each run, Pallas kernels for 0% -> 0%
where the time goes in v1:
time: 75.9 us; the launch traced here: 75.6 us
  waiting for transfers between devices  33.6 us (44%)
  matrix products  14.3 us (19%)
  starting transfers between devices  12.7 us (17%)
  local copies, waits for them, and re-layouts  9.49 us (13%)
  other arithmetic  4.95 us (7%)
    ppermute x4, waiting for transfers between devices, shifted(): return lax.ppermute(value, axis, pairs)  21.1 us
    all_to_all x1, waiting for transfers between devices, shards(): lax.all_to_all(jnp.stack(jnp.split(mixed, lax.axis_size('energy'), axis=2...  12.5 us
    ppermute x4, starting transfers between devices, shifted(): return lax.ppermute(value, axis, pairs)  8.99 us
    unnamed x22, local copies, waits for them, and re-layouts  7.25 us
    dot_general x36, matrix products, batched(): jnp.einsum('sab,sbc->sac', left, right, preferred_element_type=jnp.float32)  7.15 us
    dot_general x24, matrix products, batched_adjoint(): jnp.einsum('sab,scb->sac', left, right, preferred_element_type=jnp.float32)  6.3 us
    convert_element_type x2, other arithmetic, shards(): (total + weights[2] * above.astype(jnp.float32)).astype(jnp.bfloat16)  4.11 us
    all_to_all x1, starting transfers between devices, shards(): lax.all_to_all(jnp.stack(jnp.split(mixed, lax.axis_size('energy'), axis=2...  3.72 us
  transfers between devices with their start and end apart: 5, of which 4 were waited for; matrix products, arithmetic and copies ran while one was open for 13% of the time, Pallas kernels for 0%

profile of v1, /device:TPU:0, one launch (start us, length us, event | category | flops | bytes accessed | tf_op | source)
XLA Modules:
  0.0 75.6 jit_solution(10535563582874585212)
XLA Ops:
  0.0 1.8 %copy.214 = bf16[1,1,12,3,2,128,128]{6,5,2,4,3,1,0:T(8,128)(2,1)S(1)} copy(bf16[1,1,12,3,2,128,128]{6,5,4,3,2,1,0:T(8,128)(2,1)} %param.7) | data formatting | bytes 4718592 | tf_op args[0]
  1.8 0.3 slice_bitcast_fusion.6
  2.1 0.6 copy-done.1
  2.7 0.3 convolution_convert_fusion
  4.6 0.3 slice_bitcast_fusion.5
  5.9 0.3 fusion.94
  6.4 0.3 fusion.93
  6.6 0.3 convolution_subtract_fusion.2
  8.1 0.3 convolution_add_fusion.8
  8.4 0.3 convolution_add_fusion.1
  8.7 0.3 convolution_subtract_fusion.1
  8.9 0.3 convolution_add_fusion.7
  9.2 0.3 convolution_add_fusion.5
  9.5 0.3 convolution_add_fusion
  9.8 0.3 fusion.16
  10.0 0.3 convolution_add_fusion.4
  10.3 0.3 fusion.15
  10.6 5.1 %collective-permute-start.3 = (bf16[2,768,128]{2,1,0:T(8,128)(2,1)S(1)}, bf16[2,768,128]{2,1,0:T(8,128)(2,1)S(1)}, u32[]{:S(2)}, u32[]{:S(2)}) collective-permute-start(bf16[2,768,128]{2,1,0:T(8,128)(2,1)S(1)} %pad_maximum_fusion.1), channel_id=1, source_target_pairs={{0,3},{1,0},{2,1},{3,2},{4,7},{5,4},{6,5},{7,6},{8,11},{9,8},{10,9... | collective-permute-start | bytes 1179656 | tf_op jit(solution)/shard_map/ppermute | solution.py:10
  18.0 0.3 fusion.91
  18.2 0.3 convolution_subtract_fusion.8
  20.2 0.3 convolution_add_fusion.18
  20.5 0.3 convolution_add_fusion.11
  20.8 0.3 convolution_subtract_fusion.7
  21.0 0.3 convolution_add_fusion.17
  21.3 0.3 convolution_add_fusion.15
  21.5 0.3 convolution_add_fusion.10
  21.8 0.3 fusion.8
  22.1 0.3 convolution_add_fusion.14
  22.4 0.3 fusion.7
  22.7 3.9 %collective-permute-start.1 = (bf16[2,768,128]{2,1,0:T(8,128)(2,1)S(1)}, bf16[2,768,128]{2,1,0:T(8,128)(2,1)S(1)}, u32[]{:S(2)}, u32[]{:S(2)}) collective-permute-start(bf16[2,768,128]{2,1,0:T(8,128)(2,1)S(1)} %pad_maximum_fusion), channel_id=1, source_target_pairs={{0,3},{1,0},{2,1},{3,2},{4,7},{5,4},{6,5},{7,6},{8,11},{9,8},{10,9... | collective-permute-start | bytes 1179656 | tf_op jit(solution)/shard_map/ppermute | solution.py:10
  26.6 0.6 fusion.68
  27.2 7.5 %collective-permute-done.2 = bf16[2,768,128]{2,1,0:T(8,128)(2,1)S(1)} collective-permute-done((bf16[2,768,128]{2,1,0:T(8,128)(2,1)S(1)}, bf16[2,768,128]{2,1,0:T(8,128)(2,1)S(1)}, u32[]{:S(2)}, u32[]{:S(2)}) %collective-permute-start.2) | collective-permute-done | bytes 393248 | tf_op jit(solution)/shard_map/ppermute | solution.py:10
  34.6 2.1 %add_convert_fusion = bf16[2,768,128]{2,1,0:T(8,128)(2,1)S(1)} fusion(bf16[2,768,128]{2,1,0:T(8,128)(2,1)S(1)} %collective-permute-done.3, bf16[2,768,128]{2,1,0:T(8,128)(2,1)S(1)} %collective-permute-done.2, f32[]{:T(128)} %get-tuple-element.6, f32[]{:T(128)} %get-tuple-element.7, f32[]{:T(128)} %get-tuple-element.5, bf16[1,768,128]{2,1,0:T(8,128)(2,1)S(1)} %bitcast.282, ...), kind=kLoop, calls=%fused_computation.71 | loop fusion | flops 1966080 | bytes 1572876 | tf_op jit(solution)/shard_map/convert_element_type | solution.py:79
  36.7 5.5 %collective-permute-done.1 = bf16[2,768,128]{2,1,0:T(8,128)(2,1)S(1)} collective-permute-done((bf16[2,768,128]{2,1,0:T(8,128)(2,1)S(1)}, bf16[2,768,128]{2,1,0:T(8,128)(2,1)S(1)}, u32[]{:S(2)}, u32[]{:S(2)}) %collective-permute-start.1) | collective-permute-done | bytes 393248 | tf_op jit(solution)/shard_map/ppermute | solution.py:10
  42.1 8.2 %collective-permute-done = bf16[2,768,128]{2,1,0:T(8,128)(2,1)S(1)} collective-permute-done((bf16[2,768,128]{2,1,0:T(8,128)(2,1)S(1)}, bf16[2,768,128]{2,1,0:T(8,128)(2,1)S(1)}, u32[]{:S(2)}, u32[]{:S(2)}) %collective-permute-start) | collective-permute-done | bytes 393248 | tf_op jit(solution)/shard_map/ppermute | solution.py:10
  50.3 2.1 %add_convert_fusion.1 = bf16[2,768,128]{2,1,0:T(8,128)(2,1)S(1)} fusion(bf16[2,768,128]{2,1,0:T(8,128)(2,1)S(1)} %collective-permute-done.1, bf16[2,768,128]{2,1,0:T(8,128)(2,1)S(1)} %collective-permute-done, f32[]{:T(128)} %get-tuple-element.6, f32[]{:T(128)} %get-tuple-element.7, f32[]{:T(128)} %get-tuple-element.5, bf16[1,768,128]{2,1,0:T(8,128)(2,1)S(1)} %bitcast.286, ...), kind=kLoop, calls=%fused_computation.72 | loop fusion | flops 1966080 | bytes 1572876 | tf_op jit(solution)/shard_map/convert_element_type | solution.py:79
  52.5 0.6 fusion.52
  53.1 0.6 fusion.51
  53.8 0.6 fusion.50
  54.4 0.6 fusion.49
  55.1 0.6 fusion.48
  55.7 0.6 fusion.47
  56.4 0.6 fusion.46
  57.0 0.6 fusion.45
  57.6 3.7 %all-to-all-start = ((bf16[8,1,2,192,128]{4,3,2,1,0:T(8,128)(2,1)}), bf16[8,1,2,192,128]{4,3,2,1,0:T(8,128)(2,1)S(1)}, u32[]{:S(2)}, u32[]{:S(2)}) async-start(bf16[8,1,2,192,128]{4,3,2,1,0:T(8,128)(2,1)} %fusion.45), calls=%async_computation | async-start | bytes 1572864 | tf_op jit(solution)/shard_map/all_to_all | solution.py:86
  61.5 12.5 %all-to-all-done = bf16[8,1,2,192,128]{4,3,2,1,0:T(8,128)(2,1)S(1)} async-done(((bf16[8,1,2,192,128]{4,3,2,1,0:T(8,128)(2,1)}), bf16[8,1,2,192,128]{4,3,2,1,0:T(8,128)(2,1)S(1)}, u32[]{:S(2)}, u32[]{:S(2)}) %all-to-all-start) | async-done | bytes 786464 | tf_op jit(solution)/shard_map/all_to_all | solution.py:86
  74.0 0.5 fusion
  74.5 1.0 %copy.150 = bf16[8,1,2,192,128]{4,3,2,1,0:T(8,128)(2,1)} copy(bf16[8,1,2,192,128]{4,0,3,2,1:T(8,128)(2,1)S(1)} %fusion) | data formatting | bytes 1572864 | tf_op jit(solution)/shard_map/broadcast_in_dim | solution.py:93
  (58 shorter events, 7.9 us)
Async XLA Ops:
  1.8 0.9 %copy-start.1 = (bf16[4,128,128]{2,1,0:T(8,128)(2,1)S(1)}, bf16[4,128,128]{2,1,0:T(8,128)(2,1)}, u32[]{:S(2)}) copy-start(bf16[4,128,128]{2,1,0:T(8,128)(2,1)} %param.9) | copy-start | bytes 393220
  1.8 0.9 %copy-start.5 = (s32[12]{0:T(128)S(1)}, s32[12]{0:T(128)}, u32[]{:S(2)}) copy-start(s32[12]{0:T(128)} %param.10) | copy-start | bytes 148
  3.4 1.1 %copy-start = (bf16[1,1,12,2,128,128]{5,4,3,2,1,0:T(8,128)(2,1)S(1)}, bf16[1,1,12,2,128,128]{5,4,3,2,1,0:T(8,128)(2,1)}, u32[]{:S(2)}) copy-start(bf16[1,1,12,2,128,128]{5,4,3,2,1,0:T(8,128)(2,1)} %param.8) | copy-start | bytes 2359300
  10.6 16.6 %collective-permute-start.3 = (bf16[2,768,128]{2,1,0:T(8,128)(2,1)S(1)}, bf16[2,768,128]{2,1,0:T(8,128)(2,1)S(1)}, u32[]{:S(2)}, u32[]{:S(2)}) collective-permute-start(bf16[2,768,128]{2,1,0:T(8,128)(2,1)S(1)} %pad_maximum_fusion.1), channel_id=1, source_target_pairs={{0,3},{1,0},{2,1},{3,2},{4,7},{5,4},{6,5},{7,6},{8,11},{9,8},{10,9... | collective-permute-start | bytes 1179656 | tf_op jit(solution)/shard_map/ppermute | solution.py:10
  15.7 18.9 %collective-permute-start.2 = (bf16[2,768,128]{2,1,0:T(8,128)(2,1)S(1)}, bf16[2,768,128]{2,1,0:T(8,128)(2,1)S(1)}, u32[]{:S(2)}, u32[]{:S(2)}) collective-permute-start(bf16[2,768,128]{2,1,0:T(8,128)(2,1)S(1)} %pad_maximum_fusion.1), channel_id=1, source_target_pairs={{0,1},{1,2},{2,3},{3,0},{4,5},{5,6},{6,7},{7,4},{8,9},{9,10},{10,1... | collective-permute-start | bytes 1179656 | tf_op jit(solution)/shard_map/ppermute | solution.py:10
  22.1 4.5 %copy-start.3 = (s32[1,3]{1,0:T(1,128)S(1)}, s32[1,3]{1,0:T(1,128)}, u32[]{:S(2)}) copy-start(s32[1,3]{1,0:T(1,128)} %param.11) | copy-start | bytes 40
  22.7 19.5 %collective-permute-start.1 = (bf16[2,768,128]{2,1,0:T(8,128)(2,1)S(1)}, bf16[2,768,128]{2,1,0:T(8,128)(2,1)S(1)}, u32[]{:S(2)}, u32[]{:S(2)}) collective-permute-start(bf16[2,768,128]{2,1,0:T(8,128)(2,1)S(1)} %pad_maximum_fusion), channel_id=1, source_target_pairs={{0,3},{1,0},{2,1},{3,2},{4,7},{5,4},{6,5},{7,6},{8,11},{9,8},{10,9... | collective-permute-start | bytes 1179656 | tf_op jit(solution)/shard_map/ppermute | solution.py:10
  26.5 23.8 %collective-permute-start = (bf16[2,768,128]{2,1,0:T(8,128)(2,1)S(1)}, bf16[2,768,128]{2,1,0:T(8,128)(2,1)S(1)}, u32[]{:S(2)}, u32[]{:S(2)}) collective-permute-start(bf16[2,768,128]{2,1,0:T(8,128)(2,1)S(1)} %pad_maximum_fusion), channel_id=1, source_target_pairs={{0,1},{1,2},{2,3},{3,0},{4,5},{5,6},{6,7},{7,4},{8,9},{9,10},{10,1... | collective-permute-start | bytes 1179656 | tf_op jit(solution)/shard_map/ppermute | solution.py:10
  52.4 8.9 %copy-start.2 = (s32[32]{0:T(128)S(1)}, s32[32]{0:T(128)}, u32[]{:S(2)}) copy-start(s32[32]{0:T(128)} %param.12) | copy-start | bytes 388
  52.5 8.9 %copy-start.4 = (f32[32]{0:T(128)S(1)}, f32[32]{0:T(128)}, u32[]{:S(2)}) copy-start(f32[32]{0:T(128)} %param.13) | copy-start | bytes 388
  57.6 16.3 %all-to-all-start = ((bf16[8,1,2,192,128]{4,3,2,1,0:T(8,128)(2,1)}), bf16[8,1,2,192,128]{4,3,2,1,0:T(8,128)(2,1)S(1)}, u32[]{:S(2)}, u32[]{:S(2)}) async-start(bf16[8,1,2,192,128]{4,3,2,1,0:T(8,128)(2,1)} %fusion.45), calls=%async_computation | async-start | bytes 1572864 | tf_op jit(solution)/shard_map/all_to_all | solution.py:86
